TPU v7x, 32 devices: a whole 2x2x4 slice. The times are simulated.
32 devices in a mesh: sec: 8 (over z, x), fld: 4 (over y, core).
Axes of the slice: x: 2, y: 2, z: 4, core: 2. Of those that a mesh axis runs over, the one named last changes fastest.
Arguments:
- surface: float32 [4, 256, 512], P('fld', 'sec'), may hold values from -6 to 6
- diffusivity: float32 [4, 256, 512], P('fld', 'sec'), may hold values from 0.02 to 0.24
- send_list: int32 [8, 8, 171], P('sec'), may hold values from 0 to 127
- recv_slot: int32 [1024, 4], P('sec'), may hold values from 0 to 1367, as said below
- weights: bfloat16 [1024, 4, 128, 128], P(('sec', 'fld')), may hold values from -0.25 to 0.25
Outputs:
- stepped: float32 [4, 256, 512], P('fld', 'sec')
- remapped: float32 [4, 256, 512], P('fld', 'sec')
Inputs may be any that keep to these rules, and one draw needn't show every extreme that they name: `recv_slot`: the 512 entries of one device's target blocks are distinct slots, all of devices of the other component; from one source device to one target device at most 171 slots are used, and that many in some pair.
All inputs are finite; a program needn't handle non-finite values.
Results may differ from a plain program's by a relative error of at most 0.0029.
Values may be sent and summed in bfloat16 or wider, within the bound.
A program may use at most 64 MiB of HBM per device.

v0:
```python
import jax
import jax.numpy as jnp
from jax import lax
from jax.sharding import PartitionSpec as P

SUBSTEPS = 4


def padded(block, sides, width):
    for axis, dim in sides:
        count = lax.axis_size(axis)
        forward = [(i, i + 1) for i in range(count - 1)]
        backward = [(target, source) for source, target in forward]
        low = lax.ppermute(
            lax.slice_in_dim(block, block.shape[dim] - width, None, axis=dim), axis, forward
        )
        high = lax.ppermute(lax.slice_in_dim(block, 0, width, axis=dim), axis, backward)
        block = jnp.concatenate([low, block, high], axis=dim)
    return block


def valid_rows(count, first, lowest, highest):
    global_row = first + jnp.arange(count, dtype=jnp.int32)
    return ((global_row >= lowest) & (global_row < highest))[None, :, None]


def update(extended, kappa):
    upper = extended[:, :-2]
    lower = extended[:, 2:]
    middle = extended[:, 1:-1]
    lap = upper + lower + jnp.roll(middle, 1, 2) + jnp.roll(middle, -1, 2) - 4.0 * middle
    return middle + kappa * lap


def per_device(surface, diffusivity, send_list, recv_slot, weights):
    sec_count = lax.axis_size("sec")
    here = lax.axis_index("sec")
    rows = surface.shape[1]
    cols = surface.shape[2]
    atmos_count = sec_count * 3 // 8
    is_ocean = here >= atmos_count
    lowest = jnp.where(is_ocean, atmos_count * rows, 0)
    highest = jnp.where(is_ocean, sec_count * rows, atmos_count * rows)
    field = surface
    for step in range(SUBSTEPS):
        extended = padded(field, (("sec", 1),), 1)
        inside = valid_rows(rows + 2, here * rows - 1, lowest, highest)
        extended = jnp.where(inside, extended, 0.0)
        field = update(extended, diffusivity)
    blocks = field.reshape(-1, 128).astype(jnp.bfloat16)
    outgoing = blocks[send_list[0]]
    incoming = lax.all_to_all(outgoing, "sec", split_axis=0, concat_axis=0, tiled=True)
    flat = incoming.reshape(-1, 128)
    pairs = flat[recv_slot]
    gathered = lax.all_to_all(pairs[None], "fld", split_axis=1, concat_axis=0, tiled=True)
    result = jnp.einsum("tkij,ftkj->fti", weights, gathered, preferred_element_type=jnp.float32)
    returned = lax.all_to_all(result, "fld", split_axis=0, concat_axis=1, tiled=True)
    remapped = returned.reshape(1, rows, cols)
    return (field, remapped)


def solution(mesh):
    return jax.shard_map(
        per_device,
        mesh=mesh,
        in_specs=(
            P("fld", "sec", None),
            P("fld", "sec", None),
            P("sec", None, None),
            P("sec", None),
            P(("sec", "fld"), None, None, None),
        ),
        out_specs=(P("fld", "sec", None), P("fld", "sec", None)),
        check_vma=False,
    )
```

profile of v0, /device:TPU:0, one launch (start us, length us, event | category | flops | bytes accessed | tf_op | source)
XLA Modules:
  0.0 82.4 jit_solution(17160284931847837862)
XLA Ops:
  0.6 0.7 fusion.34
  1.4 1.3 %collective-permute-start.1 = (f32[1,1,512]{2,1,0:T(1,128)S(1)}, f32[1,1,512]{2,1,0:T(1,128)S(1)}, u32[]{:S(2)}, u32[]{:S(2)}) collective-permute-start(f32[1,1,512]{2,1,0:T(1,128)S(1)} %get-tuple-element.27), channel_id=1, source_target_pairs={{4,0},{8,4},{12,8},{16,12},{20,16},{24,20},{28,24},{5,1},{9,5},{13... | collective-permute-start | bytes 6152 | tf_op jit(solution)/shard_map/ppermute | solution.py:17
  2.7 5.5 %collective-permute-start = (f32[1,1,512]{2,1,0:T(1,128)S(1)}, f32[1,1,512]{2,1,0:T(1,128)S(1)}, u32[]{:S(2)}, u32[]{:S(2)}) collective-permute-start(f32[1,1,512]{2,1,0:T(1,128)S(1)} %get-tuple-element.26), channel_id=1, source_target_pairs={{0,4},{4,8},{8,12},{12,16},{16,20},{20,24},{24,28},{1,5},{5,9},{9,... | collective-permute-start | bytes 6152 | tf_op jit(solution)/shard_map/ppermute | solution.py:14
  8.2 1.3 %collective-permute-done = f32[1,1,512]{2,1,0:T(1,128)S(1)} collective-permute-done((f32[1,1,512]{2,1,0:T(1,128)S(1)}, f32[1,1,512]{2,1,0:T(1,128)S(1)}, u32[]{:S(2)}, u32[]{:S(2)}) %collective-permute-start) | collective-permute-done | bytes 2080 | tf_op jit(solution)/shard_map/ppermute | solution.py:14
  9.4 0.9 %maximum_select_fusion = f32[1,34,512]{2,1,0:T(8,128)S(1)} fusion(f32[1,1,512]{2,1,0:T(1,128)S(1)} %collective-permute-done.1, f32[1,32,512]{2,1,0:T(8,128)} %param.5, f32[1,1,512]{2,1,0:T(1,128)S(1)} %collective-permute-done, pred[34]{0:T(512)(128)(4,1)S(1)} %compare_and_fusion), kind=kLoop, calls=%fused_computation.4 | loop fusion | flops 52224 | bytes 139298 | tf_op jit(solution)/shard_map/jit(_where)/select_n | solution.py:48
  10.5 0.9 %fusion.20 = f32[1,32,512]{2,1,0:T(8,128)S(1)} fusion(f32[1,32,512]{2,1,0:T(8,128)} %param.6, f32[1,34,512]{2,1,0:T(8,128)S(1)} %maximum_select_fusion, f32[1,32,511]{2,1,0:T(8,128)S(1)} %get-tuple-element.17, f32[1,32,1]{2,1,0:T(8,128)S(1)} %get-tuple-element.19, f32[1,32,1]{2,1,0:T(8,128)S(1)} %get-tuple-element.18, f32[1,32,511]{2,1,0:T(8,128)S(1)} %get-tuple-element.16), kind=kLoop, calls=%fused_computation.31 | loop fusion | flops 147456 | bytes 458752 | tf_op jit(solution)/shard_map/add | solution.py:32
  11.5 1.3 %collective-permute-start.3 = (f32[1,1,512]{2,1,0:T(1,128)S(1)}, f32[1,1,512]{2,1,0:T(1,128)S(1)}, u32[]{:S(2)}, u32[]{:S(2)}) collective-permute-start(f32[1,1,512]{2,1,0:T(1,128)S(1)} %get-tuple-element.25), channel_id=1, source_target_pairs={{4,0},{8,4},{12,8},{16,12},{20,16},{24,20},{28,24},{5,1},{9,5},{13... | collective-permute-start | bytes 6152 | tf_op jit(solution)/shard_map/ppermute | solution.py:17
  12.8 5.4 %collective-permute-start.2 = (f32[1,1,512]{2,1,0:T(1,128)S(1)}, f32[1,1,512]{2,1,0:T(1,128)S(1)}, u32[]{:S(2)}, u32[]{:S(2)}) collective-permute-start(f32[1,1,512]{2,1,0:T(1,128)S(1)} %get-tuple-element.24), channel_id=1, source_target_pairs={{0,4},{4,8},{8,12},{12,16},{16,20},{20,24},{24,28},{1,5},{5,9},{9,... | collective-permute-start | bytes 6152 | tf_op jit(solution)/shard_map/ppermute | solution.py:14
  18.2 1.3 %collective-permute-done.2 = f32[1,1,512]{2,1,0:T(1,128)S(1)} collective-permute-done((f32[1,1,512]{2,1,0:T(1,128)S(1)}, f32[1,1,512]{2,1,0:T(1,128)S(1)}, u32[]{:S(2)}, u32[]{:S(2)}) %collective-permute-start.2) | collective-permute-done | bytes 2080 | tf_op jit(solution)/shard_map/ppermute | solution.py:14
  19.6 0.1 fusion.27
  19.8 0.9 %fusion.15 = f32[1,32,512]{2,1,0:T(8,128)S(1)} fusion(f32[1,32,512]{2,1,0:T(8,128)} %param.6, f32[1,34,512]{2,1,0:T(8,128)S(1)} %maximum_select_fusion.1, f32[1,32,511]{2,1,0:T(8,128)S(1)} %get-tuple-element.13, f32[1,32,1]{2,1,0:T(8,128)S(1)} %get-tuple-element.15, f32[1,32,1]{2,1,0:T(8,128)S(1)} %get-tuple-element.14, f32[1,32,511]{2,1,0:T(8,128)S(1)} %get-tuple-element.12), kind=kLoop, calls=%fused_computation.25 | loop fusion | flops 147456 | bytes 458752 | tf_op jit(solution)/shard_map/add | solution.py:32
  20.7 1.3 %collective-permute-start.5 = (f32[1,1,512]{2,1,0:T(1,128)S(1)}, f32[1,1,512]{2,1,0:T(1,128)S(1)}, u32[]{:S(2)}, u32[]{:S(2)}) collective-permute-start(f32[1,1,512]{2,1,0:T(1,128)S(1)} %get-tuple-element.23), channel_id=1, source_target_pairs={{4,0},{8,4},{12,8},{16,12},{20,16},{24,20},{28,24},{5,1},{9,5},{13... | collective-permute-start | bytes 6152 | tf_op jit(solution)/shard_map/ppermute | solution.py:17
  22.0 5.7 %collective-permute-start.4 = (f32[1,1,512]{2,1,0:T(1,128)S(1)}, f32[1,1,512]{2,1,0:T(1,128)S(1)}, u32[]{:S(2)}, u32[]{:S(2)}) collective-permute-start(f32[1,1,512]{2,1,0:T(1,128)S(1)} %get-tuple-element.22), channel_id=1, source_target_pairs={{0,4},{4,8},{8,12},{12,16},{16,20},{20,24},{24,28},{1,5},{5,9},{9,... | collective-permute-start | bytes 6152 | tf_op jit(solution)/shard_map/ppermute | solution.py:14
  27.7 0.7 compare_select_fusion
  28.5 0.5 collective-permute-done.4
  29.3 0.9 %fusion.10 = f32[1,32,512]{2,1,0:T(8,128)S(1)} fusion(f32[1,32,512]{2,1,0:T(8,128)} %param.6, f32[1,34,512]{2,1,0:T(8,128)S(1)} %maximum_select_fusion.2, f32[1,32,511]{2,1,0:T(8,128)S(1)} %get-tuple-element.9, f32[1,32,1]{2,1,0:T(8,128)S(1)} %get-tuple-element.11, f32[1,32,1]{2,1,0:T(8,128)S(1)} %get-tuple-element.10, f32[1,32,511]{2,1,0:T(8,128)S(1)} %get-tuple-element.8), kind=kLoop, calls=%fused_computation.19 | loop fusion | flops 147456 | bytes 458752 | tf_op jit(solution)/shard_map/add | solution.py:32
  30.2 1.3 %collective-permute-start.7 = (f32[1,1,512]{2,1,0:T(1,128)S(1)}, f32[1,1,512]{2,1,0:T(1,128)S(1)}, u32[]{:S(2)}, u32[]{:S(2)}) collective-permute-start(f32[1,1,512]{2,1,0:T(1,128)S(1)} %get-tuple-element.21), channel_id=1, source_target_pairs={{4,0},{8,4},{12,8},{16,12},{20,16},{24,20},{28,24},{5,1},{9,5},{13... | collective-permute-start | bytes 6152 | tf_op jit(solution)/shard_map/ppermute | solution.py:17
  31.5 5.7 %collective-permute-start.6 = (f32[1,1,512]{2,1,0:T(1,128)S(1)}, f32[1,1,512]{2,1,0:T(1,128)S(1)}, u32[]{:S(2)}, u32[]{:S(2)}) collective-permute-start(f32[1,1,512]{2,1,0:T(1,128)S(1)} %get-tuple-element.20), channel_id=1, source_target_pairs={{0,4},{4,8},{8,12},{12,16},{16,20},{20,24},{24,28},{1,5},{5,9},{9,... | collective-permute-start | bytes 6152 | tf_op jit(solution)/shard_map/ppermute | solution.py:14
  37.3 1.3 %collective-permute-done.6 = f32[1,1,512]{2,1,0:T(1,128)S(1)} collective-permute-done((f32[1,1,512]{2,1,0:T(1,128)S(1)}, f32[1,1,512]{2,1,0:T(1,128)S(1)}, u32[]{:S(2)}, u32[]{:S(2)}) %collective-permute-start.6) | collective-permute-done | bytes 2080 | tf_op jit(solution)/shard_map/ppermute | solution.py:14
  38.8 1.6 %fusion.21 = (bf16[1,32,512]{2,1,0:T(8,128)(2,1)S(1)}, f32[1,32,512]{2,1,0:T(8,128)}) fusion(f32[1,32,512]{2,1,0:T(8,128)} %param.6, f32[1,32,1]{2,1,0:T(8,128)S(1)} %get-tuple-element.5, f32[1,32,511]{2,1,0:T(8,128)S(1)} %get-tuple-element.7, f32[1,32,511]{2,1,0:T(8,128)S(1)} %get-tuple-element.6, f32[1,32,1]{2,1,0:T(8,128)S(1)} %get-tuple-element.4, ...), kind=kLoop, calls=%fused_computation.37 | loop fusion | flops 163840 | bytes 491520 | tf_op jit(solution)/shard_map/convert_element_type | solution.py:50
  40.4 3.3 %gather_fusion = bf16[1368,128]{1,0:T(8,128)(2,1)S(1)} fusion(bf16[128,128]{1,0:T(8,128)(2,1)S(1)} %convert_element_type.7, s32[2048]{0:T(1024)S(1)} %pad_clamp_fusion), kind=kCustom, calls=%fused_computation | custom fusion | bytes 705888 | tf_op jit(solution)/shard_map/gather | solution.py:51
  43.7 0.8 %reshape.295 = bf16[8,171,128]{2,1,0:T(8,128)(2,1)} reshape(bf16[1368,128]{1,0:T(8,128)(2,1)S(1)} %gather_fusion) | data formatting | bytes 700416 | tf_op jit(solution)/shard_map/gather | solution.py:51
  44.5 9.7 %all-to-all-start = ((bf16[8,171,128]{2,1,0:T(8,128)(2,1)}), bf16[8,171,128]{2,1,0:T(8,128)(2,1)S(1)}, u32[]{:S(2)}, u32[]{:S(2)}) async-start(bf16[8,171,128]{2,1,0:T(8,128)(2,1)} %reshape.295), calls=%async_computation | async-start | bytes 720896 | tf_op jit(solution)/shard_map/all_to_all | solution.py:52
  54.3 0.1 copy.11
  54.4 0.1 reshape.304
  54.5 8.7 %all-to-all-done = bf16[8,171,128]{2,1,0:T(8,128)(2,1)S(1)} async-done(((bf16[8,171,128]{2,1,0:T(8,128)(2,1)}), bf16[8,171,128]{2,1,0:T(8,128)(2,1)S(1)}, u32[]{:S(2)}, u32[]{:S(2)}) %all-to-all-start) | async-done | bytes 350240 | tf_op jit(solution)/shard_map/all_to_all | solution.py:52
  63.2 0.1 reshape.292
  63.3 1.3 %gather_fusion.1 = bf16[512,128]{1,0:T(8,128)(2,1)S(1)} fusion(bf16[1368,128]{1,0:T(8,128)(2,1)S(1)} %reshape.292, s32[1024]{0:T(1024)S(1)} %pad_clamp_fusion.1), kind=kCustom, calls=%fused_computation.1 | custom fusion | bytes 264192 | tf_op jit(solution)/shard_map/gather | solution.py:54
  64.7 7.2 %all_to_all.26 = bf16[1,128,4,128]{3,2,0,1:T(4,128)(2,1)S(1)} all-to-all(bf16[1,128,4,128]{3,2,0,1:T(4,128)(2,1)S(1)} %bitcast.14), channel_id=1, replica_groups=mesh['sec'=8,'fld'=4] {'fld'}, dimensions={1} | all-to-all | bytes 262144 | tf_op jit(solution)/shard_map/all_to_all | solution.py:55
  71.9 3.4 %convolution_bitcast_fusion = f32[4,32,128]{2,0,1:T(4,128)S(1)} fusion(bf16[32,4,128,128]{3,2,1,0:T(8,128)(2,1)} %param.9, bf16[4,32,4,128]{3,2,1,0:T(4,128)(2,1)S(1)} %bitcast.15), kind=kOutput, calls=%fused_computation.2 | convolution fusion | flops 16777216 | bytes 4390912 | tf_op jit(solution)/shard_map/tkij,ftkj->fti/dot_general | solution.py:56
  75.3 6.5 %all_to_all.27 = f32[4,32,128]{2,1,0:T(8,128)S(1)} all-to-all(f32[4,32,128]{2,1,0:T(8,128)S(1)} %copy.15), channel_id=1, replica_groups=mesh['sec'=8,'fld'=4] {'fld'}, dimensions={0} | all-to-all | bytes 131072 | tf_op jit(solution)/shard_map/all_to_all | solution.py:57
  81.8 0.6 reshape.293
  (26 shorter events, 1.0 us)
Async XLA Ops:
  1.4 6.8 %collective-permute-start.1 = (f32[1,1,512]{2,1,0:T(1,128)S(1)}, f32[1,1,512]{2,1,0:T(1,128)S(1)}, u32[]{:S(2)}, u32[]{:S(2)}) collective-permute-start(f32[1,1,512]{2,1,0:T(1,128)S(1)} %get-tuple-element.27), channel_id=1, source_target_pairs={{4,0},{8,4},{12,8},{16,12},{20,16},{24,20},{28,24},{5,1},{9,5},{13... | collective-permute-start | bytes 6152 | tf_op jit(solution)/shard_map/ppermute | solution.py:17
  2.7 6.8 %collective-permute-start = (f32[1,1,512]{2,1,0:T(1,128)S(1)}, f32[1,1,512]{2,1,0:T(1,128)S(1)}, u32[]{:S(2)}, u32[]{:S(2)}) collective-permute-start(f32[1,1,512]{2,1,0:T(1,128)S(1)} %get-tuple-element.26), channel_id=1, source_target_pairs={{0,4},{4,8},{8,12},{12,16},{16,20},{20,24},{24,28},{1,5},{5,9},{9,... | collective-permute-start | bytes 6152 | tf_op jit(solution)/shard_map/ppermute | solution.py:14
  10.4 43.8 %copy-start = (s32[128,4]{0,1:T(4,128)S(1)}, s32[128,4]{0,1:T(4,128)}, u32[]{:S(2)}) copy-start(s32[128,4]{0,1:T(4,128)} %param.8) | copy-start | bytes 6148
  11.5 6.8 %collective-permute-start.3 = (f32[1,1,512]{2,1,0:T(1,128)S(1)}, f32[1,1,512]{2,1,0:T(1,128)S(1)}, u32[]{:S(2)}, u32[]{:S(2)}) collective-permute-start(f32[1,1,512]{2,1,0:T(1,128)S(1)} %get-tuple-element.25), channel_id=1, source_target_pairs={{4,0},{8,4},{12,8},{16,12},{20,16},{24,20},{28,24},{5,1},{9,5},{13... | collective-permute-start | bytes 6152 | tf_op jit(solution)/shard_map/ppermute | solution.py:17
  12.8 6.7 %collective-permute-start.2 = (f32[1,1,512]{2,1,0:T(1,128)S(1)}, f32[1,1,512]{2,1,0:T(1,128)S(1)}, u32[]{:S(2)}, u32[]{:S(2)}) collective-permute-start(f32[1,1,512]{2,1,0:T(1,128)S(1)} %get-tuple-element.24), channel_id=1, source_target_pairs={{0,4},{4,8},{8,12},{12,16},{16,20},{20,24},{24,28},{1,5},{5,9},{9,... | collective-permute-start | bytes 6152 | tf_op jit(solution)/shard_map/ppermute | solution.py:14
  20.7 7.8 %collective-permute-start.5 = (f32[1,1,512]{2,1,0:T(1,128)S(1)}, f32[1,1,512]{2,1,0:T(1,128)S(1)}, u32[]{:S(2)}, u32[]{:S(2)}) collective-permute-start(f32[1,1,512]{2,1,0:T(1,128)S(1)} %get-tuple-element.23), channel_id=1, source_target_pairs={{4,0},{8,4},{12,8},{16,12},{20,16},{24,20},{28,24},{5,1},{9,5},{13... | collective-permute-start | bytes 6152 | tf_op jit(solution)/shard_map/ppermute | solution.py:17
  22.0 7.0 %collective-permute-start.4 = (f32[1,1,512]{2,1,0:T(1,128)S(1)}, f32[1,1,512]{2,1,0:T(1,128)S(1)}, u32[]{:S(2)}, u32[]{:S(2)}) collective-permute-start(f32[1,1,512]{2,1,0:T(1,128)S(1)} %get-tuple-element.22), channel_id=1, source_target_pairs={{0,4},{4,8},{8,12},{12,16},{16,20},{20,24},{24,28},{1,5},{5,9},{9,... | collective-permute-start | bytes 6152 | tf_op jit(solution)/shard_map/ppermute | solution.py:14
  30.2 7.0 %collective-permute-start.7 = (f32[1,1,512]{2,1,0:T(1,128)S(1)}, f32[1,1,512]{2,1,0:T(1,128)S(1)}, u32[]{:S(2)}, u32[]{:S(2)}) collective-permute-start(f32[1,1,512]{2,1,0:T(1,128)S(1)} %get-tuple-element.21), channel_id=1, source_target_pairs={{4,0},{8,4},{12,8},{16,12},{20,16},{24,20},{28,24},{5,1},{9,5},{13... | collective-permute-start | bytes 6152 | tf_op jit(solution)/shard_map/ppermute | solution.py:17
  31.5 7.0 %collective-permute-start.6 = (f32[1,1,512]{2,1,0:T(1,128)S(1)}, f32[1,1,512]{2,1,0:T(1,128)S(1)}, u32[]{:S(2)}, u32[]{:S(2)}) collective-permute-start(f32[1,1,512]{2,1,0:T(1,128)S(1)} %get-tuple-element.20), channel_id=1, source_target_pairs={{0,4},{4,8},{8,12},{12,16},{16,20},{20,24},{24,28},{1,5},{5,9},{9,... | collective-permute-start | bytes 6152 | tf_op jit(solution)/shard_map/ppermute | solution.py:14
  44.5 18.7 %all-to-all-start = ((bf16[8,171,128]{2,1,0:T(8,128)(2,1)}), bf16[8,171,128]{2,1,0:T(8,128)(2,1)S(1)}, u32[]{:S(2)}, u32[]{:S(2)}) async-start(bf16[8,171,128]{2,1,0:T(8,128)(2,1)} %reshape.295), calls=%async_computation | async-start | bytes 720896 | tf_op jit(solution)/shard_map/all_to_all | solution.py:52
where the time goes:
time: 83.2 us; the launch traced here: 82.4 us
  starting transfers between devices  37.2 us (45%)
  blocking collectives  13.7 us (16%)
  waiting for transfers between devices  13 us (16%)
  local copies, waits for them, and re-layouts  8.01 us (10%)
  other arithmetic  6.24 us (8%)
  matrix products  3.38 us (4%)
  between operations  0.88 us (1%)
    ppermute x4, starting transfers between devices, padded(): lax.ppermute(lax.slice_in_dim(block, block.shape[dim] - width, None, axis...  22.3 us
    all_to_all x1, starting transfers between devices, per_device(): lax.all_to_all(outgoing, 'sec', split_axis=0, concat_axis=0, tiled=True)  9.72 us
    all_to_all x1, waiting for transfers between devices, per_device(): lax.all_to_all(outgoing, 'sec', split_axis=0, concat_axis=0, tiled=True)  8.69 us
    all_to_all x1, blocking collectives, per_device(): lax.all_to_all(pairs[None], 'fld', split_axis=1, concat_axis=0, tiled=True)  7.22 us
    all_to_all x1, blocking collectives, per_device(): lax.all_to_all(result, 'fld', split_axis=0, concat_axis=1, tiled=True)  6.49 us
    ppermute x4, starting transfers between devices, padded(): lax.ppermute(lax.slice_in_dim(block, 0, width, axis=dim), axis, backward)  5.16 us
    ppermute x4, waiting for transfers between devices, padded(): lax.ppermute(lax.slice_in_dim(block, block.shape[dim] - width, None, axis...  4.29 us
    gather x2, local copies, waits for them, and re-layouts, per_device(): outgoing = blocks[send_list[0]]  4.17 us
  transfers between devices with their start and end apart: 9, of which 5 were waited for; matrix products, arithmetic and copies ran while one was open for 1% of the time, Pallas kernels for 0%

commit v1 on v0

v1 whole, which is shorter than its diff:
```python
import functools

import jax
import jax.numpy as jnp
from jax import lax
from jax.experimental import pallas as pl
from jax.experimental.pallas import tpu as pltpu
from jax.sharding import PartitionSpec as P

SUBSTEPS = 4
EDGE = 8
MESH = pl.DeviceIdType.MESH
F32 = jnp.float32
BF16 = jnp.bfloat16


def diffuse(u, kappa):
    rows, cols = u.shape
    for _ in range(SUBSTEPS):
        around = (
            pltpu.roll(u, 1, 0)
            + pltpu.roll(u, rows - 1, 0)
            + pltpu.roll(u, 1, 1)
            + pltpu.roll(u, cols - 1, 1)
        )
        u = u + kappa * (around - 4.0 * u)
    return u


def columns_of(x, width):
    return jnp.concatenate(
        [x[:, c : c + width] for c in range(0, x.shape[1], width)], axis=0
    )


def block_ids(shape, rows, per_row):
    inner = rows - EDGE
    p = lax.broadcasted_iota(jnp.int32, shape, 0)
    ids = jnp.zeros(shape, jnp.int32)
    for c in range(per_row):
        start = c * inner
        row = p - start + SUBSTEPS
        ids = jnp.where((p >= start) & (p < start + inner), row * per_row + c, ids)
        start = per_row * inner + c * EDGE
        row = p - start
        row = jnp.where(row < SUBSTEPS, row, row + inner)
        ids = jnp.where((p >= start) & (p < start + EDGE), row * per_row + c, ids)
    return ids


def kernel(
    n_sec, n_fld, surf, kap, sl, rst, w_hbm, stepped, remapped,
    halo, wv, sl_in, blk, land, cmat, acc, gbf, gath, xs, ys, ret, back, res,
    w_sem, halo_send, halo_recv, sl_send, sl_recv, in_send, in_recv,
    ed_send, ed_recv, g_send, g_recv, r_send, r_recv,
):
    rows, cols = surf.shape[1], surf.shape[2]
    width = wv.shape[3]
    per_row = cols // width
    n_blk = rows * per_row
    n_inner = (rows - EDGE) * per_row
    cap = sl.shape[2]
    n_k, n_t = rst.shape
    t_loc = n_t // n_fld

    me_s = lax.axis_index("sec")
    me_f = lax.axis_index("fld")
    atmos = n_sec * 3 // 8
    is_ocean = me_s >= atmos
    own_base = jnp.where(is_ocean, atmos, 0)
    own_end = jnp.where(is_ocean, n_sec, atmos)
    oth_base = jnp.where(is_ocean, 0, atmos)
    n_oth = jnp.where(is_ocean, atmos, n_sec - atmos)
    has_up = me_s > own_base
    has_dn = me_s < own_end - 1
    mine = me_s - own_base

    w_copy = pltpu.make_async_copy(w_hbm, wv, w_sem)
    w_copy.start()

    barrier = pltpu.get_barrier_semaphore()

    @pl.when(has_up)
    def _():
        pl.semaphore_signal(barrier, 1, device_id={"sec": me_s - 1, "fld": me_f}, device_id_type=MESH)

    @pl.when(has_dn)
    def _():
        pl.semaphore_signal(barrier, 1, device_id={"sec": me_s + 1, "fld": me_f}, device_id_type=MESH)

    @pl.loop(0, n_oth)
    def _(j):
        pl.semaphore_signal(barrier, 1, device_id={"sec": oth_base + j, "fld": me_f}, device_id_type=MESH)

    for i in range(1, n_fld):
        pl.semaphore_signal(
            barrier, 1, device_id={"sec": me_s, "fld": lax.rem(me_f + i, n_fld)}, device_id_type=MESH
        )

    inner = diffuse(surf[0], kap[0])[SUBSTEPS : rows - SUBSTEPS]
    stepped[0, SUBSTEPS : rows - SUBSTEPS, :] = inner
    blk[0:n_inner, :] = columns_of(inner, width).astype(BF16)

    pl.semaphore_wait(
        barrier, n_oth + has_up.astype(jnp.int32) + has_dn.astype(jnp.int32) + (n_fld - 1)
    )

    def halo_copy(which, side):
        ref = (surf, kap)[which]
        first, to = ((rows - EDGE, me_s + 1), (0, me_s - 1))[side]
        return pltpu.make_async_remote_copy(
            src_ref=ref.at[0, pl.ds(first, EDGE), :],
            dst_ref=halo.at[which, side],
            send_sem=halo_send.at[which, side],
            recv_sem=halo_recv.at[which, side],
            device_id={"sec": to, "fld": me_f},
            device_id_type=MESH,
        )

    @pl.when(has_dn)
    def _():
        halo_copy(0, 0).start()
        halo_copy(1, 0).start()

    @pl.when(has_up)
    def _():
        halo_copy(0, 1).start()
        halo_copy(1, 1).start()

    def sl_copy(j, slot):
        target = oth_base + j
        return pltpu.make_async_remote_copy(
            src_ref=sl.at[0, pl.ds(pl.multiple_of(target // 8 * 8, 8), 8), :],
            dst_ref=sl_in.at[slot],
            send_sem=sl_send.at[j],
            recv_sem=sl_recv.at[slot],
            device_id={"sec": target, "fld": me_f},
            device_id_type=MESH,
        )

    def block_copy(j, slot, edge):
        part = pl.ds(n_inner, n_blk - n_inner) if edge else pl.ds(0, n_inner)
        return pltpu.make_async_remote_copy(
            src_ref=blk.at[part],
            dst_ref=land.at[slot, part],
            send_sem=(ed_send if edge else in_send).at[j],
            recv_sem=(ed_recv if edge else in_recv).at[slot],
            device_id={"sec": oth_base + j, "fld": me_f},
            device_id_type=MESH,
        )

    @pl.loop(0, n_oth)
    def _(j):
        sl_copy(j, mine).start()

    @pl.loop(0, n_oth)
    def _(j):
        block_copy(j, mine, False).start()

    @pl.when(has_up)
    def _():
        halo_copy(0, 0).wait_recv()
        halo_copy(1, 0).wait_recv()

    @pl.when(jnp.logical_not(has_up))
    def _():
        halo[:, 0] = jnp.zeros((2, EDGE, cols), F32)

    @pl.when(has_dn)
    def _():
        halo_copy(0, 1).wait_recv()
        halo_copy(1, 1).wait_recv()

    @pl.when(jnp.logical_not(has_dn))
    def _():
        halo[:, 1] = jnp.zeros((2, EDGE, cols), F32)

    def around_edges(which):
        ref = (surf, kap)[which]
        return jnp.concatenate(
            [halo[which, 0], ref[0, 0:EDGE, :], ref[0, rows - EDGE : rows, :], halo[which, 1]], axis=0
        )

    edges = diffuse(around_edges(0), around_edges(1))
    top, bottom = edges[EDGE : 2 * EDGE], edges[2 * EDGE : 3 * EDGE]
    upper = lax.broadcasted_iota(jnp.int32, (EDGE, cols), 0) < SUBSTEPS
    edge = jnp.where(upper, top, bottom)
    stepped[0, 0:SUBSTEPS, :] = edge[0:SUBSTEPS]
    stepped[0, rows - SUBSTEPS : rows, :] = edge[SUBSTEPS:EDGE]
    blk[n_inner:n_blk, :] = columns_of(edge, width).astype(BF16)

    @pl.loop(0, n_oth)
    def _(j):
        block_copy(j, mine, True).start()

    ids = block_ids((n_blk, cap), rows, per_row)
    slot_of = lax.broadcasted_iota(jnp.int32, (cap, n_t), 0)

    @pl.loop(0, n_oth)
    def _(j):
        sl_copy(j, j).wait_recv()
        sent = sl_in[j, pl.ds(lax.rem(me_s, 8), 1), :]
        pick = jnp.where(ids == sent, 1.0, 0.0).astype(BF16)
        slots = slot_of + (oth_base + j) * cap
        for k in range(n_k):
            put = jnp.where(rst[k : k + 1, :] == slots, 1.0, 0.0).astype(BF16)
            chosen = jnp.dot(pick, put, preferred_element_type=F32)
            cmat[j, k * n_t : (k + 1) * n_t, :] = chosen.T.astype(BF16)

    acc[...] = jnp.zeros_like(acc)

    @pl.loop(0, n_oth)
    def _(j):
        block_copy(j, j, False).wait_recv()
        block_copy(j, j, True).wait_recv()
        acc[...] += jnp.dot(cmat[j], land[j], preferred_element_type=F32)

    for k in range(n_k):
        gbf[k] = acc[k * n_t : (k + 1) * n_t, :].astype(BF16)

    def pair_copy(i, slot):
        to = lax.rem(me_f + i, n_fld)
        return pltpu.make_async_remote_copy(
            src_ref=gbf.at[:, pl.ds(pl.multiple_of(to * t_loc, t_loc), t_loc), :],
            dst_ref=gath.at[slot],
            send_sem=g_send.at[i],
            recv_sem=g_recv.at[i],
            device_id={"sec": me_s, "fld": to},
            device_id_type=MESH,
        )

    for i in range(1, n_fld):
        pair_copy(i, me_f).start()
    gath[me_f] = gbf[:, pl.ds(pl.multiple_of(me_f * t_loc, t_loc), t_loc), :]
    w_copy.wait()
    for i in range(1, n_fld):
        pair_copy(i, lax.rem(me_f + n_fld - i, n_fld)).wait_recv()

    for f in range(n_fld):
        for k in range(n_k):
            xs[k, pl.ds(f, t_loc, stride=n_fld), :] = gath[f, k].astype(F32)

    group = 8 // n_fld
    which_t = lax.broadcasted_iota(jnp.int32, (8, width), 0) // n_fld

    def remap(g, carry):
        at = pl.multiple_of(g * 8, 8)
        x = jnp.concatenate([xs[k, pl.ds(at, 8), :] for k in range(n_k)], axis=1).astype(BF16)
        y = jnp.zeros((8, width), F32)
        for u in range(group):
            w = jnp.concatenate([wv[g * group + u, k] for k in range(n_k)], axis=1)
            full = lax.dot_general(x, w, (((1,), (1,)), ((), ())), preferred_element_type=F32)
            y = jnp.where(which_t == u, full, y)
        ys[pl.ds(at, 8), :] = y
        return carry

    lax.fori_loop(0, t_loc // group, remap, 0, unroll=4)

    for f in range(n_fld):
        ret[f] = ys[pl.ds(f, t_loc, stride=n_fld), :].astype(BF16)

    def return_copy(i, slot):
        to = lax.rem(me_f + i, n_fld)
        return pltpu.make_async_remote_copy(
            src_ref=ret.at[to],
            dst_ref=back.at[slot],
            send_sem=r_send.at[i],
            recv_sem=r_recv.at[i],
            device_id={"sec": me_s, "fld": to},
            device_id_type=MESH,
        )

    for i in range(1, n_fld):
        return_copy(i, me_f).start()
    back[me_f] = ret[me_f]
    for i in range(1, n_fld):
        return_copy(i, lax.rem(me_f + n_fld - i, n_fld)).wait_recv()
    for q in range(n_fld):
        res[q * t_loc : (q + 1) * t_loc, :] = back[q].astype(F32)
    for c in range(per_row):
        remapped[0, :, c * width : (c + 1) * width] = res[pl.ds(c, rows, stride=per_row), :]

    @pl.when(has_dn)
    def _():
        halo_copy(0, 0).wait_send()
        halo_copy(1, 0).wait_send()

    @pl.when(has_up)
    def _():
        halo_copy(0, 1).wait_send()
        halo_copy(1, 1).wait_send()

    @pl.loop(0, n_oth)
    def _(j):
        sl_copy(j, mine).wait_send()
        block_copy(j, mine, False).wait_send()
        block_copy(j, mine, True).wait_send()

    for i in range(1, n_fld):
        pair_copy(i, me_f).wait_send()
        return_copy(i, me_f).wait_send()


def per_device(n_sec, n_fld, surface, diffusivity, send_list, recv_slot, weights):
    _, rows, cols = surface.shape
    t_loc, n_k, width, _ = weights.shape
    n_t = recv_slot.shape[0]
    n_blk = rows * cols // width
    cap = send_list.shape[2]
    most = n_sec - n_sec * 3 // 8
    vmem = pl.BlockSpec(memory_space=pltpu.VMEM)
    dma = pltpu.SemaphoreType.DMA
    shape = jax.ShapeDtypeStruct(surface.shape, F32)
    return pl.pallas_call(
        functools.partial(kernel, n_sec, n_fld),
        out_shape=(shape, shape),
        in_specs=[vmem, vmem, vmem, vmem, pl.BlockSpec(memory_space=pl.ANY)],
        out_specs=(vmem, vmem),
        scratch_shapes=[
            pltpu.VMEM((2, 2, EDGE, cols), F32),
            pltpu.VMEM(weights.shape, BF16),
            pltpu.VMEM((most, 8, cap), jnp.int32),
            pltpu.VMEM((n_blk, width), BF16),
            pltpu.VMEM((most, n_blk, width), BF16),
            pltpu.VMEM((most, n_k * n_t, n_blk), BF16),
            pltpu.VMEM((n_k * n_t, width), F32),
            pltpu.VMEM((n_k, n_t, width), BF16),
            pltpu.VMEM((n_fld, n_k, t_loc, width), BF16),
            pltpu.VMEM((n_k, t_loc * n_fld, width), F32),
            pltpu.VMEM((t_loc * n_fld, width), F32),
            pltpu.VMEM((n_fld, t_loc, width), BF16),
            pltpu.VMEM((n_fld, t_loc, width), BF16),
            pltpu.VMEM((n_blk, width), F32),
            dma,
            dma((2, 2)),
            dma((2, 2)),
            dma((most,)),
            dma((most,)),
            dma((most,)),
            dma((most,)),
            dma((most,)),
            dma((most,)),
            dma((n_fld,)),
            dma((n_fld,)),
            dma((n_fld,)),
            dma((n_fld,)),
        ],
        compiler_params=pltpu.CompilerParams(
            collective_id=0, has_side_effects=True, vmem_limit_bytes=48 * 1024 * 1024
        ),
    )(surface, diffusivity, send_list, recv_slot.T, weights)


def solution(mesh):
    return jax.shard_map(
        functools.partial(per_device, mesh.shape["sec"], mesh.shape["fld"]),
        mesh=mesh,
        in_specs=(
            P("fld", "sec", None),
            P("fld", "sec", None),
            P("sec", None, None),
            P("sec", None),
            P(("sec", "fld"), None, None, None),
        ),
        out_specs=(P("fld", "sec", None), P("fld", "sec", None)),
        check_vma=False,
    )
```

time: 83.2 us -> 28.8 us (0.35)
  starting transfers between devices: 37.2 us -> 0 us
  Pallas kernels: 0 us -> 21.4 us
  blocking collectives: 13.7 us -> 0 us
  waiting for transfers between devices: 13 us -> 0 us
  other arithmetic: 6.24 us -> 0 us
  matrix products: 3.38 us -> 0 us
  local copies, waits for them, and re-layouts: 8.01 us -> 6.5 us
    ppermute x8 -> x0, starting transfers between devices: 27.5 us -> none  [the longest x4 22.3 us: padded(): lax.ppermute(lax.slice_in_dim(block, block.shape[dim] - width, None, axis...]
    pallas_call x0 -> x1, Pallas kernels: none -> 21.4 us  [per_device(): pl.pallas_call(functools.partial(kernel, n_sec, n_fld), out_shape=(shape,...]
    all_to_all x2 -> x0, blocking collectives: 13.7 us -> none  [the longest x1 7.22 us: per_device(): lax.all_to_all(pairs[None], 'fld', split_axis=1, concat_axis=0, tiled=True)]
    all_to_all x1 -> x0, starting transfers between devices: 9.72 us -> none  [per_device(): lax.all_to_all(outgoing, 'sec', split_axis=0, concat_axis=0, tiled=True)]
    all_to_all x1 -> x0, waiting for transfers between devices: 8.69 us -> none  [per_device(): lax.all_to_all(outgoing, 'sec', split_axis=0, concat_axis=0, tiled=True)]
    unnamed x2 -> x12, local copies, waits for them, and re-layouts: 0.01 us -> 6.5 us
    gather x3 -> x0, local copies, waits for them, and re-layouts: 5.51 us -> none  [the longest x2 4.17 us: per_device(): outgoing = blocks[send_list[0]]]
    ppermute x8 -> x0, waiting for transfers between devices: 4.3 us -> none  [the longest x4 4.29 us: padded(): lax.ppermute(lax.slice_in_dim(block, block.shape[dim] - width, None, axis...]
  transfers between devices with their start and end apart: 9 -> 0, of which waited for: 5 -> 0; matrix products, arithmetic and copies ran while one was open for 1% -> 0% of each run, Pallas kernels for 0% -> 0%
where the time goes in v1:
time: 28.8 us; the launch traced here: 28.5 us
  Pallas kernels  21.4 us (74%)
  local copies, waits for them, and re-layouts  6.5 us (23%)
  between operations  0.65 us (2%)
    pallas_call x1, Pallas kernels, per_device(): pl.pallas_call(functools.partial(kernel, n_sec, n_fld), out_shape=(shape,...  21.4 us
    unnamed x12, local copies, waits for them, and re-layouts  6.5 us

profile of v1, /device:TPU:0, one launch (start us, length us, event | category | flops | bytes accessed | tf_op | source)
XLA Modules:
  0.0 28.5 jit_solution(758732585366166371)
XLA Ops:
  0.6 0.0 copy-start
  0.6 2.2 %copy-done = bf16[32,4,128,128]{3,2,1,0:T(8,128)(2,1)S(1)} copy-done((bf16[32,4,128,128]{3,2,1,0:T(8,128)(2,1)S(1)}, bf16[32,4,128,128]{3,2,1,0:T(8,128)(2,1)}, u32[]{:S(2)}) %copy-start) | copy-done | bytes 4194328
  2.8 0.0 copy-start.1
  2.8 0.8 %copy-done.1 = f32[1,32,512]{2,1,0:T(8,128)S(1)} copy-done((f32[1,32,512]{2,1,0:T(8,128)S(1)}, f32[1,32,512]{2,1,0:T(8,128)}, u32[]{:S(2)}) %copy-start.1) | copy-done | bytes 65560
  3.7 0.0 copy-start.2
  3.7 0.8 %copy-done.2 = f32[1,32,512]{2,1,0:T(8,128)S(1)} copy-done((f32[1,32,512]{2,1,0:T(8,128)S(1)}, f32[1,32,512]{2,1,0:T(8,128)}, u32[]{:S(2)}) %copy-start.2) | copy-done | bytes 65560
  4.5 0.0 copy-start.3
  4.5 0.7 %copy-done.3 = s32[1,8,171]{2,1,0:T(8,128)S(1)} copy-done((s32[1,8,171]{2,1,0:T(8,128)S(1)}, s32[1,8,171]{2,1,0:T(8,128)}, u32[]{:S(2)}) %copy-start.3) | copy-done | bytes 5496
  5.2 0.0 copy-start.4
  5.2 0.7 %copy-done.4 = s32[128,4]{0,1:T(4,128)S(1)} copy-done((s32[128,4]{0,1:T(4,128)S(1)}, s32[128,4]{0,1:T(4,128)}, u32[]{:S(2)}) %copy-start.4) | copy-done | bytes 2072
  5.9 21.4 %shard_map.68 = (f32[1,32,512]{2,1,0:T(8,128)S(1)}, f32[1,32,512]{2,1,0:T(8,128)S(1)}) custom-call(f32[1,32,512]{2,1,0:T(8,128)S(1)} %copy-done.1, f32[1,32,512]{2,1,0:T(8,128)S(1)} %copy-done.2, s32[1,8,171]{2,1,0:T(8,128)S(1)} %copy-done.3, s32[4,128]{1,0:T(4,128)S(1)} %bitcast.1, bf16[32,4,128,128]{3,2,1,0:T(8,128)(2,1)S(1)} %copy-done), custom_call_target="tpu_custom_call" | custom-call | tf_op jit(solution)/shard_map/pallas_call | solution.py:314
  27.3 0.6 %copy.9 = f32[1,32,512]{2,1,0:T(8,128)} copy(f32[1,32,512]{2,1,0:T(8,128)S(1)} %get-tuple-element.4) | data formatting | bytes 131072
  27.9 0.6 %copy.10 = f32[1,32,512]{2,1,0:T(8,128)} copy(f32[1,32,512]{2,1,0:T(8,128)S(1)} %get-tuple-element.5) | data formatting | bytes 131072
Async XLA Ops:
  0.6 2.2 %copy-start = (bf16[32,4,128,128]{3,2,1,0:T(8,128)(2,1)S(1)}, bf16[32,4,128,128]{3,2,1,0:T(8,128)(2,1)}, u32[]{:S(2)}) copy-start(bf16[32,4,128,128]{3,2,1,0:T(8,128)(2,1)} %w_hbm.1) | copy-start | bytes 12582916
  2.8 0.8 %copy-start.1 = (f32[1,32,512]{2,1,0:T(8,128)S(1)}, f32[1,32,512]{2,1,0:T(8,128)}, u32[]{:S(2)}) copy-start(f32[1,32,512]{2,1,0:T(8,128)} %surf.1) | copy-start | bytes 196612
  3.7 0.8 %copy-start.2 = (f32[1,32,512]{2,1,0:T(8,128)S(1)}, f32[1,32,512]{2,1,0:T(8,128)}, u32[]{:S(2)}) copy-start(f32[1,32,512]{2,1,0:T(8,128)} %kap.1) | copy-start | bytes 196612
  4.5 0.7 %copy-start.3 = (s32[1,8,171]{2,1,0:T(8,128)S(1)}, s32[1,8,171]{2,1,0:T(8,128)}, u32[]{:S(2)}) copy-start(s32[1,8,171]{2,1,0:T(8,128)} %sl.1) | copy-start | bytes 16420
  5.2 0.7 %copy-start.4 = (s32[128,4]{0,1:T(4,128)S(1)}, s32[128,4]{0,1:T(4,128)}, u32[]{:S(2)}) copy-start(s32[128,4]{0,1:T(4,128)} %param.8) | copy-start | bytes 6148

commit v2 on v1

--- a/solution.py
+++ b/solution.py
@@ -49,9 +49,9 @@
 
 
 def kernel(
-    n_sec, n_fld, surf, kap, sl, rst, w_hbm, stepped, remapped,
-    halo, wv, sl_in, blk, land, cmat, acc, gbf, gath, xs, ys, ret, back, res,
-    w_sem, halo_send, halo_recv, sl_send, sl_recv, in_send, in_recv,
+    n_sec, n_fld, surf_hbm, kap_hbm, sl_hbm, rst_hbm, w_hbm, stepped, remapped,
+    surf, kap, sl, rst, halo, wv, sl_in, blk, land, cmat, acc, gbf, gath, xs, ys, ret, back, res,
+    load_sem, halo_send, halo_recv, sl_send, sl_recv, in_send, in_recv,
     ed_send, ed_recv, g_send, g_recv, r_send, r_recv,
 ):
     rows, cols = surf.shape[1], surf.shape[2]
@@ -75,8 +75,14 @@
     has_dn = me_s < own_end - 1
     mine = me_s - own_base
 
-    w_copy = pltpu.make_async_copy(w_hbm, wv, w_sem)
-    w_copy.start()
+    loads = [
+        pltpu.make_async_copy(src, dst, load_sem.at[i])
+        for i, (src, dst) in enumerate(
+            ((surf_hbm, surf), (kap_hbm, kap), (sl_hbm, sl), (rst_hbm, rst), (w_hbm, wv))
+        )
+    ]
+    for load in loads:
+        load.start()
 
     barrier = pltpu.get_barrier_semaphore()
 
@@ -97,10 +103,14 @@
             barrier, 1, device_id={"sec": me_s, "fld": lax.rem(me_f + i, n_fld)}, device_id_type=MESH
         )
 
+    loads[0].wait()
+    loads[1].wait()
     inner = diffuse(surf[0], kap[0])[SUBSTEPS : rows - SUBSTEPS]
     stepped[0, SUBSTEPS : rows - SUBSTEPS, :] = inner
     blk[0:n_inner, :] = columns_of(inner, width).astype(BF16)
 
+    loads[2].wait()
+    loads[3].wait()
     pl.semaphore_wait(
         barrier, n_oth + has_up.astype(jnp.int32) + has_dn.astype(jnp.int32) + (n_fld - 1)
     )
@@ -232,7 +242,7 @@
     for i in range(1, n_fld):
         pair_copy(i, me_f).start()
     gath[me_f] = gbf[:, pl.ds(pl.multiple_of(me_f * t_loc, t_loc), t_loc), :]
-    w_copy.wait()
+    loads[4].wait()
     for i in range(1, n_fld):
         pair_copy(i, lax.rem(me_f + n_fld - i, n_fld)).wait_recv()
 
@@ -314,9 +324,13 @@
     return pl.pallas_call(
         functools.partial(kernel, n_sec, n_fld),
         out_shape=(shape, shape),
-        in_specs=[vmem, vmem, vmem, vmem, pl.BlockSpec(memory_space=pl.ANY)],
+        in_specs=[pl.BlockSpec(memory_space=pltpu.HBM)] * 5,
         out_specs=(vmem, vmem),
         scratch_shapes=[
+            pltpu.VMEM(surface.shape, F32),
+            pltpu.VMEM(surface.shape, F32),
+            pltpu.VMEM(send_list.shape, jnp.int32),
+            pltpu.VMEM((n_k, n_t), jnp.int32),
             pltpu.VMEM((2, 2, EDGE, cols), F32),
             pltpu.VMEM(weights.shape, BF16),
             pltpu.VMEM((most, 8, cap), jnp.int32),
@@ -331,7 +345,7 @@
             pltpu.VMEM((n_fld, t_loc, width), BF16),
             pltpu.VMEM((n_fld, t_loc, width), BF16),
             pltpu.VMEM((n_blk, width), F32),
-            dma,
+            dma((5,)),
             dma((2, 2)),
             dma((2, 2)),
             dma((most,)),
@@ -346,7 +360,7 @@
             dma((n_fld,)),
         ],
         compiler_params=pltpu.CompilerParams(
-            collective_id=0, has_side_effects=True, vmem_limit_bytes=48 * 1024 * 1024
+            collective_id=0, has_side_effects=True, vmem_limit_bytes=63 * 1024 * 1024
         ),
     )(surface, diffusivity, send_list, recv_slot.T, weights)
 

time: 28.8 us -> 25.7 us (0.89)
  local copies, waits for them, and re-layouts: 6.5 us -> 2.95 us
  Pallas kernels: 21.4 us -> 21.9 us
    unnamed x12 -> x2, local copies, waits for them, and re-layouts: 6.5 us -> 2.95 us
    pallas_call x1, Pallas kernels: 21.4 us -> 21.9 us  [per_device(): pl.pallas_call(functools.partial(kernel, n_sec, n_fld), out_shape=(shape,...]
where the time goes in v2:
time: 25.7 us; the launch traced here: 25.5 us
  Pallas kernels  21.9 us (85%)
  local copies, waits for them, and re-layouts  2.95 us (11%)
  between operations  0.64 us (2%)
    pallas_call x1, Pallas kernels, per_device(): pl.pallas_call(functools.partial(kernel, n_sec, n_fld), out_shape=(shape,...  21.9 us
    unnamed x2, local copies, waits for them, and re-layouts  2.95 us

profile of v2, /device:TPU:0, one launch (start us, length us, event | category | flops | bytes accessed | tf_op | source)
XLA Modules:
  0.0 25.5 jit_solution(18233268633150285590)
XLA Ops:
  0.6 21.9 %shard_map.68 = (f32[1,32,512]{2,1,0:T(8,128)}, f32[1,32,512]{2,1,0:T(8,128)}) custom-call(f32[1,32,512]{2,1,0:T(8,128)} %surf_hbm.1, f32[1,32,512]{2,1,0:T(8,128)} %kap_hbm.1, s32[1,8,171]{2,1,0:T(8,128)} %sl_hbm.1, s32[4,128]{1,0:T(4,128)} %bitcast.1, bf16[32,4,128,128]{3,2,1,0:T(8,128)(2,1)} %w_hbm.1), custom_call_target="tpu_custom_call" | custom-call | tf_op jit(solution)/shard_map/pallas_call | solution.py:324
  22.5 1.5 %copy.9 = f32[1,32,512]{2,1,0:T(8,128)} copy(f32[1,32,512]{2,1,0:T(8,128)} %get-tuple-element.4) | data formatting | bytes 131072
  24.0 1.5 %copy.10 = f32[1,32,512]{2,1,0:T(8,128)} copy(f32[1,32,512]{2,1,0:T(8,128)} %get-tuple-element.5) | data formatting | bytes 131072

commit v3 on v2

--- a/solution.py
+++ b/solution.py
@@ -49,7 +49,7 @@
 
 
 def kernel(
-    n_sec, n_fld, surf_hbm, kap_hbm, sl_hbm, rst_hbm, w_hbm, stepped, remapped,
+    n_sec, n_fld, surf_hbm, kap_hbm, sl_hbm, rst_hbm, w_hbm, out,
     surf, kap, sl, rst, halo, wv, sl_in, blk, land, cmat, acc, gbf, gath, xs, ys, ret, back, res,
     load_sem, halo_send, halo_recv, sl_send, sl_recv, in_send, in_recv,
     ed_send, ed_recv, g_send, g_recv, r_send, r_recv,
@@ -106,7 +106,7 @@
     loads[0].wait()
     loads[1].wait()
     inner = diffuse(surf[0], kap[0])[SUBSTEPS : rows - SUBSTEPS]
-    stepped[0, SUBSTEPS : rows - SUBSTEPS, :] = inner
+    out[0, SUBSTEPS : rows - SUBSTEPS, :] = inner
     blk[0:n_inner, :] = columns_of(inner, width).astype(BF16)
 
     loads[2].wait()
@@ -195,8 +195,8 @@
     top, bottom = edges[EDGE : 2 * EDGE], edges[2 * EDGE : 3 * EDGE]
     upper = lax.broadcasted_iota(jnp.int32, (EDGE, cols), 0) < SUBSTEPS
     edge = jnp.where(upper, top, bottom)
-    stepped[0, 0:SUBSTEPS, :] = edge[0:SUBSTEPS]
-    stepped[0, rows - SUBSTEPS : rows, :] = edge[SUBSTEPS:EDGE]
+    out[0, 0:SUBSTEPS, :] = edge[0:SUBSTEPS]
+    out[0, rows - SUBSTEPS : rows, :] = edge[SUBSTEPS:EDGE]
     blk[n_inner:n_blk, :] = columns_of(edge, width).astype(BF16)
 
     @pl.loop(0, n_oth)
@@ -288,7 +288,7 @@
     for q in range(n_fld):
         res[q * t_loc : (q + 1) * t_loc, :] = back[q].astype(F32)
     for c in range(per_row):
-        remapped[0, :, c * width : (c + 1) * width] = res[pl.ds(c, rows, stride=per_row), :]
+        out[1, :, c * width : (c + 1) * width] = res[pl.ds(c, rows, stride=per_row), :]
 
     @pl.when(has_dn)
     def _():
@@ -320,12 +320,12 @@
     most = n_sec - n_sec * 3 // 8
     vmem = pl.BlockSpec(memory_space=pltpu.VMEM)
     dma = pltpu.SemaphoreType.DMA
-    shape = jax.ShapeDtypeStruct(surface.shape, F32)
-    return pl.pallas_call(
+    operands = [pltpu.with_memory_space_constraint(x, pltpu.HBM) for x in (surface, diffusivity, send_list, recv_slot.T, weights)]
+    both = pl.pallas_call(
         functools.partial(kernel, n_sec, n_fld),
-        out_shape=(shape, shape),
+        out_shape=pltpu.VMEM((2, rows, cols), F32),
         in_specs=[pl.BlockSpec(memory_space=pltpu.HBM)] * 5,
-        out_specs=(vmem, vmem),
+        out_specs=vmem,
         scratch_shapes=[
             pltpu.VMEM(surface.shape, F32),
             pltpu.VMEM(surface.shape, F32),
@@ -360,9 +360,10 @@
             dma((n_fld,)),
         ],
         compiler_params=pltpu.CompilerParams(
-            collective_id=0, has_side_effects=True, vmem_limit_bytes=63 * 1024 * 1024
+            collective_id=0, has_side_effects=True, vmem_limit_bytes=48 * 1024 * 1024
         ),
-    )(surface, diffusivity, send_list, recv_slot.T, weights)
+    )(*operands)
+    return both[0:1], both[1:2]
 
 
 def solution(mesh):

time: 25.7 us -> 22.7 us (0.88)
  local copies, waits for them, and re-layouts: 2.95 us -> 0.66 us
  Pallas kernels: 21.9 us -> 21.2 us
    unnamed x2 -> x0, local copies, waits for them, and re-layouts: 2.95 us -> none
    slice x0 -> x1, local copies, waits for them, and re-layouts: none -> 0.66 us  [per_device(): return (both[0:1], both[1:2])]
    pallas_call x1, Pallas kernels: 21.9 us -> 21.2 us  [per_device(): pl.pallas_call(functools.partial(kernel, n_sec, n_fld), out_shape=pltpu.V...]
where the time goes in v3:
time: 22.7 us; the launch traced here: 22.5 us
  Pallas kernels  21.2 us (93%)
  local copies, waits for them, and re-layouts  0.66 us (3%)
  between operations  0.64 us (3%)
    pallas_call x1, Pallas kernels, per_device(): pl.pallas_call(functools.partial(kernel, n_sec, n_fld), out_shape=pltpu.V...  21.2 us
    slice x1, local copies, waits for them, and re-layouts, per_device(): return (both[0:1], both[1:2])  0.66 us

profile of v3, /device:TPU:0, one launch (start us, length us, event | category | flops | bytes accessed | tf_op | source)
XLA Modules:
  0.0 22.5 jit_solution(3470120020051335428)
XLA Ops:
  0.6 21.2 %shard_map.68 = f32[2,32,512]{2,1,0:T(8,128)S(1)} custom-call(f32[1,32,512]{2,1,0:T(8,128)} %surf_hbm.1, f32[1,32,512]{2,1,0:T(8,128)} %kap_hbm.1, s32[1,8,171]{2,1,0:T(8,128)} %sl_hbm.1, s32[4,128]{1,0:T(4,128)} %bitcast.1, bf16[32,4,128,128]{3,2,1,0:T(8,128)(2,1)} %w_hbm.1), custom_call_target="tpu_custom_call" | custom-call | tf_op jit(solution)/shard_map/pallas_call | solution.py:324
  21.9 0.7 %fusion = (f32[1,32,512]{2,1,0:T(8,128)}, f32[1,32,512]{2,1,0:T(8,128)}) fusion(f32[2,32,512]{2,1,0:T(8,128)S(1)} %shard_map.68), kind=kLoop, calls=%fused_computation | loop fusion | bytes 262144 | tf_op jit(solution)/shard_map/slice | solution.py:366

commit v4 on v3

--- a/solution.py
+++ b/solution.py
@@ -50,7 +50,7 @@
 
 def kernel(
     n_sec, n_fld, surf_hbm, kap_hbm, sl_hbm, rst_hbm, w_hbm, out,
-    surf, kap, sl, rst, halo, wv, sl_in, blk, land, cmat, acc, gbf, gath, xs, ys, ret, back, res,
+    surf, kap, sl, rst, halo, wv, sl_in, blk, land, cmat, asked, acc, gbf, gath, xs, ys, ret, back, res,
     load_sem, halo_send, halo_recv, sl_send, sl_recv, in_send, in_recv,
     ed_send, ed_recv, g_send, g_recv, r_send, r_recv,
 ):
@@ -111,6 +111,10 @@
 
     loads[2].wait()
     loads[3].wait()
+    for k in range(n_k):
+        row = jnp.broadcast_to(rst[k : k + 1, :].astype(F32), (width, n_t))
+        asked[k * n_t : (k + 1) * n_t, :] = row.T
+
     pl.semaphore_wait(
         barrier, n_oth + has_up.astype(jnp.int32) + has_dn.astype(jnp.int32) + (n_fld - 1)
     )
@@ -204,18 +208,18 @@
         block_copy(j, mine, True).start()
 
     ids = block_ids((n_blk, cap), rows, per_row)
-    slot_of = lax.broadcasted_iota(jnp.int32, (cap, n_t), 0)
+    slot_of = lax.broadcasted_iota(jnp.int32, (n_k * n_t, cap), 1)
 
     @pl.loop(0, n_oth)
     def _(j):
         sl_copy(j, j).wait_recv()
         sent = sl_in[j, pl.ds(lax.rem(me_s, 8), 1), :]
         pick = jnp.where(ids == sent, 1.0, 0.0).astype(BF16)
-        slots = slot_of + (oth_base + j) * cap
-        for k in range(n_k):
-            put = jnp.where(rst[k : k + 1, :] == slots, 1.0, 0.0).astype(BF16)
-            chosen = jnp.dot(pick, put, preferred_element_type=F32)
-            cmat[j, k * n_t : (k + 1) * n_t, :] = chosen.T.astype(BF16)
+        wanted = jnp.concatenate([asked[...]] * pl.cdiv(cap, width), axis=1)[:, :cap]
+        slots = (slot_of + (oth_base + j) * cap).astype(F32)
+        put = jnp.where(wanted == slots, 1.0, 0.0).astype(BF16)
+        chosen = lax.dot_general(put, pick, (((1,), (1,)), ((), ())), preferred_element_type=F32)
+        cmat[j] = chosen.astype(BF16)
 
     acc[...] = jnp.zeros_like(acc)
 
@@ -264,7 +268,7 @@
         ys[pl.ds(at, 8), :] = y
         return carry
 
-    lax.fori_loop(0, t_loc // group, remap, 0, unroll=4)
+    lax.fori_loop(0, t_loc // group, remap, 0, unroll=16)
 
     for f in range(n_fld):
         ret[f] = ys[pl.ds(f, t_loc, stride=n_fld), :].astype(BF16)
@@ -338,6 +342,7 @@
             pltpu.VMEM((most, n_blk, width), BF16),
             pltpu.VMEM((most, n_k * n_t, n_blk), BF16),
             pltpu.VMEM((n_k * n_t, width), F32),
+            pltpu.VMEM((n_k * n_t, width), F32),
             pltpu.VMEM((n_k, n_t, width), BF16),
             pltpu.VMEM((n_fld, n_k, t_loc, width), BF16),
             pltpu.VMEM((n_k, t_loc * n_fld, width), F32),

time: 22.7 us -> 22 us (0.969)
  Pallas kernels: 21.2 us -> 20.6 us
    pallas_call x1, Pallas kernels: 21.2 us -> 20.6 us  [per_device(): pl.pallas_call(functools.partial(kernel, n_sec, n_fld), out_shape=pltpu.V...]
where the time goes in v4:
time: 22 us; the launch traced here: 21.9 us
  Pallas kernels  20.6 us (94%)
  local copies, waits for them, and re-layouts  0.66 us (3%)
  between operations  0.64 us (3%)
    pallas_call x1, Pallas kernels, per_device(): pl.pallas_call(functools.partial(kernel, n_sec, n_fld), out_shape=pltpu.V...  20.6 us
    slice x1, local copies, waits for them, and re-layouts, per_device(): return (both[0:1], both[1:2])  0.66 us

profile of v4, /device:TPU:0, one launch (start us, length us, event | category | flops | bytes accessed | tf_op | source)
XLA Modules:
  0.0 21.9 jit_solution(298574441798800461)
XLA Ops:
  0.6 20.6 %shard_map.68 = f32[2,32,512]{2,1,0:T(8,128)S(1)} custom-call(f32[1,32,512]{2,1,0:T(8,128)} %surf_hbm.1, f32[1,32,512]{2,1,0:T(8,128)} %kap_hbm.1, s32[1,8,171]{2,1,0:T(8,128)} %sl_hbm.1, s32[4,128]{1,0:T(4,128)} %bitcast.1, bf16[32,4,128,128]{3,2,1,0:T(8,128)(2,1)} %w_hbm.1), custom_call_target="tpu_custom_call" | custom-call | tf_op jit(solution)/shard_map/pallas_call | solution.py:328
  21.2 0.7 %fusion = (f32[1,32,512]{2,1,0:T(8,128)}, f32[1,32,512]{2,1,0:T(8,128)}) fusion(f32[2,32,512]{2,1,0:T(8,128)S(1)} %shard_map.68), kind=kLoop, calls=%fused_computation | loop fusion | bytes 262144 | tf_op jit(solution)/shard_map/slice | solution.py:371
